TPU v7x, 32 devices: a whole 2x2x4 slice. The times are simulated.
32 devices in a mesh: dp: 16 (over z, x, core), tensor: 2 (over y).
Axes of the slice: x: 2, y: 2, z: 4, core: 2. Of those that a mesh axis runs over, the one named last changes fastest.
Arguments:
- tokens: bfloat16 [16, 1376, 1024], P('dp', 'tensor'), may hold values from -16 to 16
- cotangent: bfloat16 [16, 1376, 1024], P('dp', 'tensor'), may hold values from -6 to 6
- lengths: int32 [16], P('dp'), may hold values from 0 to 1370, as said below
- adapter_ids: int32 [16], P('dp'), may hold values from 0 to 7
- gain_one: float32 [1024], replicated, may hold values from 0.25 to 1.75
- gain_two: float32 [1024], replicated, may hold values from 0.25 to 1.75
- scale_one: float32 [1024], replicated, may hold values from 0.5 to 2
- scale_two: float32 [1024], replicated, may hold values from 0.5 to 2
- w_qkv: bfloat16 [1024, 3, 1024], P(None, None, 'tensor'), may hold values from -0.1875 to 0.1875
- w_out: bfloat16 [1024, 1024], P('tensor'), may hold values from -1 to 1
- w_up: bfloat16 [1024, 4096], P(None, 'tensor'), may hold values from -0.1875 to 0.1875
- w_down: bfloat16 [4096, 1024], P('tensor'), may hold values from -0.09375 to 0.09375
- qkv_a: bfloat16 [8, 16, 1024], replicated, may hold values from -0.1875 to 0.1875
- qkv_b: bfloat16 [8, 3, 1024, 16], P(None, None, 'tensor'), may hold values from -1.5 to 1.5
- out_a: bfloat16 [8, 16, 1024], P(None, None, 'tensor'), may hold values from -1 to 1
- out_b: bfloat16 [8, 1024, 16], replicated, may hold values from -1.5 to 1.5
- up_a: bfloat16 [8, 16, 1024], replicated, may hold values from -0.1875 to 0.1875
- up_b: bfloat16 [8, 4096, 16], P(None, 'tensor'), may hold values from -1.5 to 1.5
- down_a: bfloat16 [8, 16, 4096], P(None, None, 'tensor'), may hold values from -0.09375 to 0.09375
- down_b: bfloat16 [8, 1024, 16], replicated, may hold values from -1.5 to 1.5
Outputs:
- layer_out: bfloat16 [16, 1376, 1024], P('dp', 'tensor')
- grad_tokens: float32 [16, 1376, 1024], P('dp', 'tensor')
- grad_qkv_a: float32 [8, 16, 1024], replicated
- grad_qkv_b: float32 [8, 3, 1024, 16], P(None, None, 'tensor')
- grad_out_a: float32 [8, 16, 1024], P(None, None, 'tensor')
- grad_out_b: float32 [8, 1024, 16], replicated
- grad_up_a: float32 [8, 16, 1024], replicated
- grad_up_b: float32 [8, 4096, 16], P(None, 'tensor')
- grad_down_a: float32 [8, 16, 4096], P(None, None, 'tensor')
- grad_down_b: float32 [8, 1024, 16], replicated
Inputs may be any that keep to these rules, and one draw needn't show every extreme that they name: `lengths`: slots g * 1 to g + 1 - 1 belong to group g of the dp axis; the first c of them hold images, with c from (2) // 2 to 1, each of 685 to 1370 valid tokens, and the others are empty with length 0.
All inputs are finite; a program needn't handle non-finite values.
Results may differ from a plain program's by a relative error of at most 0.014.
The roundings to bfloat16 on the way count: a program that leaves them out, or rounds other values in their place, can miss the bound.
Values may be sent and summed in bfloat16 or wider, within the bound.
No kernel may reach another device: no remote copies, remote signals or barrier semaphores. Data moves between devices by JAX's collectives and lax.ppermute only.
A program may use at most 384 MiB of HBM per device.

v0:
```python
import jax
import jax.numpy as jnp
from jax import lax
from jax.sharding import PartitionSpec as P

HD = 64
ADAPTERS = 8
epsilon = 1e-06
masked_score = -1e30
HIGHEST = lax.Precision.HIGHEST


def product(form, left, right):
    return jnp.einsum(form, left, right, preferred_element_type=jnp.float32)


def precise(form, left, right):
    return jnp.einsum(form, left.astype(jnp.float32), right.astype(jnp.float32), precision=HIGHEST)


def select_rows(onehot, table):
    return product("sn,n...->s...", onehot, table).astype(table.dtype)


def norm_rows(values, gain_vec):
    average = jnp.mean(values, axis=-1, keepdims=True)
    centred = values - average
    variance = jnp.mean(centred * centred, axis=-1, keepdims=True)
    return centred * lax.rsqrt(variance + epsilon) * gain_vec


def norm_back(values, gain_vec, grad_normed):
    normed, pullback = jax.vjp(lambda rows: norm_rows(rows, gain_vec), values)
    return pullback(grad_normed)[0]


def gelu_slope(values):
    return (
        0.5 * (1.0 + lax.erf(values * 0.7071067811865476))
        + values * jnp.exp(-0.5 * values * values) * 0.3989422804014327
    )


def ffn_forward(rows_low, up_mat, down_mat, up_a_sel, up_b_sel, down_a_sel, down_b_sel):
    rank_up = product("std,srd->str", rows_low, up_a_sel).astype(jnp.bfloat16)
    preact = product("std,dh->sth", rows_low, up_mat) + product("str,shr->sth", rank_up, up_b_sel)
    hidden = jax.nn.gelu(preact, approximate=False).astype(jnp.bfloat16)
    rank_down = product("sth,srh->str", hidden, down_a_sel)
    terms = product("sth,hd->std", hidden, down_mat) + precise(
        "str,sdr->std", rank_down, down_b_sel
    )
    return (rank_up, preact, hidden, rank_down, terms)


def ffn_backward(
    rows_low,
    grad_rows,
    up_mat,
    down_mat,
    up_a_sel,
    up_b_sel,
    down_a_sel,
    down_b_sel,
    rank_up,
    preact,
    hidden,
    rank_down,
):
    grad_rank_down = product("std,sdr->str", grad_rows, down_b_sel).astype(jnp.bfloat16)
    grad_hidden = product("std,hd->sth", grad_rows, down_mat) + product(
        "str,srh->sth", grad_rank_down, down_a_sel
    )
    grad_preact = (grad_hidden * gelu_slope(preact)).astype(jnp.bfloat16)
    grad_up_b = product("sth,str->shr", grad_preact, rank_up)
    grad_rank_up = product("sth,shr->str", grad_preact, up_b_sel)
    grad_rows_in = product("sth,dh->std", grad_preact, up_mat) + precise(
        "str,srd->std", grad_rank_up, up_a_sel
    )
    grad_up_a = precise("str,std->srd", grad_rank_up, rows_low)
    grad_down_a = product("str,sth->srh", grad_rank_down, hidden)
    grad_down_b = precise("std,str->sdr", grad_rows, rank_down)
    return (grad_rows_in, (grad_up_a, grad_up_b, grad_down_a, grad_down_b))


def body(
    tokens,
    cotangent,
    lengths,
    adapter_ids,
    gain_one,
    gain_two,
    scale_one,
    scale_two,
    w_qkv,
    w_out,
    w_up,
    w_down,
    qkv_a,
    qkv_b,
    out_a,
    out_b,
    up_a,
    up_b,
    down_a,
    down_b,
):
    shard_rows = tokens.shape[1]
    seq_len = shard_rows * lax.axis_size("tensor")
    heads_local = w_qkv.shape[2] // HD
    scale_attn = HD ** (-0.5)
    first_row = lax.axis_index("tensor") * shard_rows
    positions = jnp.arange(seq_len, dtype=jnp.int32)
    key_valid = positions[None, :] < jnp.maximum(lengths, 1)[:, None]
    local_rows = first_row + jnp.arange(shard_rows, dtype=jnp.int32)
    row_valid = (local_rows[None, :] < lengths[:, None]).astype(jnp.float32)[:, :, None]
    adapters = jnp.arange(ADAPTERS, dtype=jnp.int32)
    onehot = (adapter_ids[:, None] == adapters[None, :]).astype(jnp.bfloat16)
    qkv_a_sel = select_rows(onehot, qkv_a)
    qkv_b_sel = select_rows(onehot, qkv_b)
    out_a_sel = select_rows(onehot, out_a)
    out_b_sel = select_rows(onehot, out_b)
    up_a_sel = select_rows(onehot, up_a)
    down_b_sel = select_rows(onehot, down_b)
    inputs = tokens.astype(jnp.float32)
    normed_one = norm_rows(inputs, gain_one).astype(jnp.bfloat16)
    full_one = lax.all_gather(normed_one, "tensor", axis=1, tiled=True)
    rank_qkv = product("std,srd->str", full_one, qkv_a_sel).astype(jnp.bfloat16)
    projected = (
        product("std,dcf->sctf", full_one, w_qkv) + product("str,scfr->sctf", rank_qkv, qkv_b_sel)
    ).astype(jnp.bfloat16)

    def split_heads(rows):
        return rows.reshape(seq_len, heads_local, HD)

    def masked_scores(queries, keyrows, valid_keys):
        scores = product("qhe,khe->hqk", queries, keyrows) * scale_attn
        return jnp.where(valid_keys[None, None, :], scores, masked_score)

    def attend(slot_items):
        slot_block, valid_keys = slot_items
        queries = split_heads(slot_block[0])
        keyrows = split_heads(slot_block[1])
        values = split_heads(slot_block[2])
        scores = masked_scores(queries, keyrows, valid_keys)
        row_max = jnp.max(scores, axis=-1, keepdims=True)
        exponent = jnp.exp(scores - row_max)
        row_total = jnp.sum(exponent, axis=-1, keepdims=True)
        soft_low = (exponent / row_total).astype(jnp.bfloat16)
        mixed_rows = (
            product("hqk,khe->qhe", soft_low, values).astype(jnp.bfloat16).reshape(seq_len, -1)
        )
        return (mixed_rows, (row_max + jnp.log(row_total))[:, :, 0])

    mixed, log_total = lax.map(attend, (projected, key_valid))
    rank_out = product("stf,srf->str", mixed, out_a_sel)
    attn_terms = product("stf,fd->std", mixed, w_out) + precise("str,sdr->std", rank_out, out_b_sel)
    attn_branch = lax.psum_scatter(attn_terms, "tensor", scatter_dimension=1, tiled=True)
    residual = inputs + scale_one * attn_branch
    normed_two = norm_rows(residual, gain_two).astype(jnp.bfloat16)
    up_mat, down_mat, up_b_all, down_a_all = (
        lax.all_gather(w_up, "tensor", axis=1, tiled=True),
        lax.all_gather(w_down, "tensor", axis=0, tiled=True),
        lax.all_gather(up_b, "tensor", axis=1, tiled=True),
        lax.all_gather(down_a, "tensor", axis=2, tiled=True),
    )
    up_b_sel = select_rows(onehot, up_b_all)
    down_a_sel = select_rows(onehot, down_a_all)
    rank_up, preact, hidden, rank_down, ffn_terms = ffn_forward(
        normed_two, up_mat, down_mat, up_a_sel, up_b_sel, down_a_sel, down_b_sel
    )
    layer_out = ((residual + scale_two * ffn_terms) * row_valid).astype(jnp.bfloat16)
    grad_out = cotangent.astype(jnp.float32) * row_valid
    grad_mlp = (scale_two * grad_out).astype(jnp.bfloat16)
    ffn_grad_in, ffn_grads = ffn_backward(
        normed_two,
        grad_mlp,
        up_mat,
        down_mat,
        up_a_sel,
        up_b_sel,
        down_a_sel,
        down_b_sel,
        rank_up,
        preact,
        hidden,
        rank_down,
    )
    grad_residual = grad_out + norm_back(residual, gain_two, ffn_grad_in)
    grad_attn = (scale_one * grad_residual).astype(jnp.bfloat16)
    full_grad_attn = lax.all_gather(grad_attn, "tensor", axis=1, tiled=True)
    grad_rank_out = product("std,sdr->str", full_grad_attn, out_b_sel).astype(jnp.bfloat16)
    grad_mixed = (
        product("std,fd->stf", full_grad_attn, w_out)
        + product("str,srf->stf", grad_rank_out, out_a_sel)
    ).astype(jnp.bfloat16)
    grad_out_a = product("str,stf->srf", grad_rank_out, mixed)
    grad_out_b = precise("std,str->sdr", full_grad_attn, rank_out)

    def attend_back(slot_items):
        slot_block, valid_keys, log_rows, grad_rows = slot_items
        queries = split_heads(slot_block[0])
        keyrows = split_heads(slot_block[1])
        values = split_heads(slot_block[2])
        scores = masked_scores(queries, keyrows, valid_keys)
        soft = jnp.exp(scores - log_rows[:, :, None])
        soft_low = soft.astype(jnp.bfloat16)
        grad_heads = split_heads(grad_rows)
        grad_soft = product("qhe,khe->hqk", grad_heads, values)
        grad_values = product("hqk,qhe->khe", soft_low, grad_heads)
        grad_scores = (
            soft * (grad_soft - jnp.sum(soft * grad_soft, axis=-1, keepdims=True))
        ).astype(jnp.bfloat16)
        grad_queries = product("hqk,khe->qhe", grad_scores, keyrows) * scale_attn
        grad_keys = product("hqk,qhe->khe", grad_scores, queries) * scale_attn
        return (
            jnp.stack([grad_queries, grad_keys, grad_values])
            .reshape(3, seq_len, -1)
            .astype(jnp.bfloat16)
        )

    grad_projected = lax.map(attend_back, (projected, key_valid, log_total, grad_mixed))
    grad_qkv_b = product("sctf,str->scfr", grad_projected, rank_qkv)
    grad_rank_qkv = product("sctf,scfr->str", grad_projected, qkv_b_sel)
    grad_one_terms = product("sctf,dcf->std", grad_projected, w_qkv) + precise(
        "str,srd->std", grad_rank_qkv, qkv_a_sel
    )
    grad_qkv_a = precise("str,std->srd", grad_rank_qkv, full_one)
    grad_normed_one = lax.psum_scatter(grad_one_terms, "tensor", scatter_dimension=1, tiled=True)
    grad_tokens = grad_residual + norm_back(inputs, gain_one, grad_normed_one)
    onehot_wide = onehot.astype(jnp.float32)

    def stack_slots(slot_grads):
        return jnp.einsum("sn,s...->n...", onehot_wide, slot_grads, precision=HIGHEST)

    grad_up_a, grad_up_b, grad_down_a, grad_down_b = ffn_grads
    sum_qkv_b, sum_out_a = lax.psum((stack_slots(grad_qkv_b), stack_slots(grad_out_a)), "dp")
    joint_sums = lax.psum(
        (
            stack_slots(grad_qkv_a),
            stack_slots(grad_out_b),
            stack_slots(grad_up_a),
            stack_slots(grad_up_b),
            stack_slots(grad_down_a),
            stack_slots(grad_down_b),
        ),
        ("dp", "tensor"),
    )
    sum_qkv_a, sum_out_b, sum_up_a, up_b_whole, down_a_whole, sum_down_b = joint_sums
    width_local = w_up.shape[1]
    first_col = lax.axis_index("tensor") * width_local
    sum_up_b = lax.dynamic_slice_in_dim(up_b_whole, first_col, width_local, 1)
    sum_down_a = lax.dynamic_slice_in_dim(down_a_whole, first_col, width_local, 2)
    return (
        layer_out,
        grad_tokens,
        sum_qkv_a,
        sum_qkv_b,
        sum_out_a,
        sum_out_b,
        sum_up_a,
        sum_up_b,
        sum_down_a,
        sum_down_b,
    )


def solution(mesh):
    return jax.shard_map(
        body,
        mesh=mesh,
        in_specs=(
            P("dp", "tensor", None),
            P("dp", "tensor", None),
            P("dp"),
            P("dp"),
            P(),
            P(),
            P(),
            P(),
            P(None, None, "tensor"),
            P("tensor", None),
            P(None, "tensor"),
            P("tensor", None),
            P(),
            P(None, None, "tensor", None),
            P(None, None, "tensor"),
            P(),
            P(),
            P(None, "tensor", None),
            P(None, None, "tensor"),
            P(),
        ),
        out_specs=(
            P("dp", "tensor", None),
            P("dp", "tensor", None),
            P(),
            P(None, None, "tensor", None),
            P(None, None, "tensor"),
            P(),
            P(),
            P(None, "tensor", None),
            P(None, None, "tensor"),
            P(),
        ),
        check_vma=False,
    )
```

profile of v0, /device:TPU:0, one launch (start us, length us, event | category | flops | bytes accessed | tf_op | source)
XLA Modules:
  0.0 1015.7 jit_solution(800403736796422366)
XLA Ops:
  22.0 35.8 %all-gather.7.cloned.1.call-done = bf16[1,1376,1024]{2,1,0:T(8,128)(2,1)} async-done(((bf16[1,688,1024]{2,1,0:T(8,128)(2,1)}), bf16[1,1376,1024]{2,1,0:T(8,128)(2,1)}) %all-gather.7.cloned.1.call-update) | async-done | bytes 2818064 | tf_op jit(solution)/shard_map/all_gather | solution.py:126
  62.9 5.6 fusion.23
  78.2 25.8 %fusion.116 = (f32[8,1376]{1,0:T(8,128)S(1)}, f32[8,1376,1376]{1,2,0:T(8,128)}) fusion(bf16[1376,8,64]{0,2,1:T(8,128)(2,1)} %bitcast.204, bf16[1376,8,64]{0,2,1:T(8,128)(2,1)} %bitcast.202, pred[1376]{0:T(1024)(128)(4,1)S(1)} %iota_compare_fusion), kind=kOutput, calls=%fused_computation.176 | convolution fusion | flops 1984247040 | bytes 63451488 | tf_op jit(solution)/shard_map/while/body/eval_jaxpr/qhe,khe->hqk/dot_general | solution.py:14
  104.1 23.7 %fusion.1 = f32[8,1376]{1,0:T(8,128)S(1)} fusion(f32[8,1376,1376]{1,2,0:T(8,128)} %get-tuple-element.63, f32[8,1376]{1,0:T(8,128)S(1)} %get-tuple-element.62), kind=kLoop, calls=%fused_computation.7 | loop fusion | flops 30283008 | bytes 60676096 | tf_op jit(solution)/shard_map/while/body/eval_jaxpr/reduce_sum | solution.py:147
  127.8 24.5 %fusion.35 = bf16[8,64,1376]{2,1,0:T(8,128)(2,1)} fusion(bf16[1376,8,64]{0,2,1:T(8,128)(2,1)} %bitcast.214, f32[8,1376,1376]{1,2,0:T(8,128)} %get-tuple-element.63, f32[8,1376]{1,0:T(8,128)S(1)} %fusion.1, f32[8,1376]{1,0:T(8,128)S(1)} %get-tuple-element.62), kind=kOutput, calls=%fused_computation.61 | convolution fusion | flops 1984962560 | bytes 63494144 | tf_op jit(solution)/shard_map/while/body/eval_jaxpr/hqk,khe->qhe/dot_general | solution.py:14
  154.0 3.4 fusion.117
  157.4 5.2 add_bitcast_fusion
  169.0 11.0 %fusion.67 = bf16[1,4096,16]{0,1,2:T(8,128)(2,1)} fusion(bf16[8,4096,16]{1,2,0:T(8,128)(2,1)} %all-gather.11.cloned.1.call-done, s32[]{:T(128)} %bitcast.198), kind=kOutput, calls=%fused_computation.100 | convolution fusion | flops 1048584 | bytes 1179652 | tf_op jit(solution)/shard_map/sn,n...->s.../dot_general | solution.py:14
  180.0 13.3 %copy.80 = bf16[1,4096,16]{1,2,0:T(8,128)(2,1)S(1)} copy(bf16[1,4096,16]{0,1,2:T(8,128)(2,1)} %fusion.67) | data formatting | bytes 262144 | tf_op jit(solution)/shard_map/sn,n...->s.../dot_general | solution.py:14
  197.3 11.8 %all-gather.13.cloned.1.call-done = bf16[4096,1024]{1,0:T(8,128)(2,1)} async-done(((bf16[2048,1024]{1,0:T(8,128)(2,1)}), bf16[4096,1024]{1,0:T(8,128)(2,1)}) %all-gather.13.cloned.1.call-update) | async-done | bytes 8388624 | tf_op jit(solution)/shard_map/all_gather | solution.py:162
  209.0 11.4 %fusion.108 = f32[688,4096]{1,0:T(8,128)} fusion(bf16[4096,1024]{1,0:T(8,128)(2,1)} %all-gather.13.cloned.1.call-done, bf16[1,688,1024]{2,1,0:T(8,128)(2,1)} %param.21, f32[1024]{0:T(1024)S(1)} %copy-done.73, f32[688]{0:T(1024)S(1)} %fusion.85), kind=kOutput, calls=%fused_computation.169 | convolution fusion | flops 5774180352 | bytes 21076672 | tf_op jit(solution)/shard_map/std,hd->sth/dot_general | solution.py:14
  220.4 60.7 %reduce-scatter.3.cloned.1.call-done = f32[1,688,1024]{2,1,0:T(8,128)} async-done(((f32[1,1376,1024]{2,1,0:T(8,128)}), f32[1,688,1024]{2,1,0:T(8,128)}) %reduce-scatter.3.cloned.1.call-update) | async-done | bytes 2818064 | tf_op jit(solution)/shard_map/reduce_scatter | solution.py:157
  287.5 99.1 %all-gather.9.cloned.1.call-done = bf16[1024,4096]{1,0:T(8,128)(2,1)} async-done(((bf16[1024,2048]{1,0:T(8,128)(2,1)}), bf16[1024,4096]{1,0:T(8,128)(2,1)}) %all-gather.9.cloned.1.call-update) | async-done | bytes 8388624 | tf_op jit(solution)/shard_map/all_gather | solution.py:161
  386.7 8.8 fusion.118
  395.5 28.7 %fusion.9 = (bf16[688,4096]{1,0:T(8,128)(2,1)S(1)}, f32[688,4096]{1,0:T(8,128)}) fusion(f32[688,4096]{1,0:T(8,128)S(1)} %fusion.118, bf16[688,16]{0,1:T(8,128)(2,1)S(1)} %copy-done.54, bf16[1,4096,16]{1,2,0:T(8,128)(2,1)S(1)} %copy.80), kind=kOutput, calls=%fused_computation.16 | convolution fusion | flops 276168704 | bytes 28333568 | tf_op jit(solution)/shard_map/str,shr->sth/dot_general | solution.py:14
  426.6 9.9 fusion.15
  439.0 8.6 fusion.120
  455.9 3.4 fusion.123
  459.3 4.1 fusion.124
  466.6 28.4 %all-gather.17.cloned.1.call-done = bf16[1,1376,1024]{2,1,0:T(8,128)(2,1)} async-done(((bf16[1,688,1024]{2,1,0:T(8,128)(2,1)}), bf16[1,1376,1024]{2,1,0:T(8,128)(2,1)}) %all-gather.17.cloned.1.call-update) | async-done | bytes 2818064 | tf_op jit(solution)/shard_map/all_gather | solution.py:190
  505.0 23.3 %fusion.29 = bf16[8,64,1376]{2,1,0:T(8,128)(2,1)} fusion(bf16[1376,8,64]{0,2,1:T(8,128)(2,1)} %bitcast.206, f32[8,1376,1376]{1,2,0:T(8,128)} %get-tuple-element.63, f32[8,1376]{1,0:T(8,128)S(1)} %copy-done.14), kind=kOutput, calls=%fused_computation.57 | convolution fusion | flops 1969815552 | bytes 63450112 | tf_op jit(solution)/shard_map/while/body/eval_jaxpr/hqk,qhe->khe/dot_general | solution.py:14
  528.3 43.5 %multiply_reduce_fusion = (f32[8,1376]{1,0:T(8,128)S(1)}, f32[8,1376,1376]{1,2,0:T(8,128)}) fusion(f32[8,1376,1376]{1,2,0:T(8,128)} %get-tuple-element.63, f32[8,1376]{1,0:T(8,128)S(1)} %copy-done.14, bf16[1376,8,64]{0,2,1:T(8,128)(2,1)} %bitcast.207, bf16[1376,8,64]{0,2,1:T(8,128)(2,1)} %bitcast.215), kind=kOutput, calls=%fused_computation.3 | convolution fusion | flops 1984247040 | bytes 124082176 | tf_op jit(solution)/shard_map/while/body/eval_jaxpr/qhe,khe->hqk/dot_general | solution.py:14
  571.8 49.0 %multiply_convert_fusion = bf16[8,1376,1376]{1,2,0:T(8,128)(2,1)} fusion(f32[8,1376,1376]{1,2,0:T(8,128)} %get-tuple-element.69, f32[8,1376,1376]{1,2,0:T(8,128)} %get-tuple-element.63, f32[8,1376]{1,0:T(8,128)S(1)} %get-tuple-element.68, f32[8,1376]{1,0:T(8,128)S(1)} %copy-done.14), kind=kLoop, calls=%fused_computation.2 | loop fusion | flops 60588032 | bytes 151558144 | tf_op jit(solution)/shard_map/while/body/eval_jaxpr/convert_element_type | solution.py:212
  620.8 16.5 %fusion.34 = bf16[8,64,1376]{2,1,0:T(8,128)(2,1)} fusion(bf16[1376,8,64]{0,2,1:T(8,128)(2,1)} %bitcast.205, bf16[8,1376,1376]{1,2,0:T(8,128)(2,1)} %multiply_convert_fusion), kind=kOutput, calls=%fused_computation.60 | convolution fusion | flops 1940226048 | bytes 33112064 | tf_op jit(solution)/shard_map/while/body/eval_jaxpr/hqk,qhe->khe/dot_general | solution.py:14
  637.4 16.5 %fusion.33 = bf16[8,64,1376]{2,1,0:T(8,128)(2,1)} fusion(bf16[1376,8,64]{0,2,1:T(8,128)(2,1)} %bitcast.203, bf16[8,1376,1376]{1,2,0:T(8,128)(2,1)} %multiply_convert_fusion), kind=kOutput, calls=%fused_computation.59 | convolution fusion | flops 1940226048 | bytes 33112064 | tf_op jit(solution)/shard_map/while/body/eval_jaxpr/hqk,khe->qhe/dot_general | solution.py:14
  661.7 3.1 fusion.40
  671.1 6.3 fusion.111
  677.4 5.0 fusion.24
  682.5 10.7 %fusion.119 = f32[688,1024]{1,0:T(8,128)S(1)} fusion(bf16[688,4096]{1,0:T(8,128)(2,1)} %copy-done.9, bf16[4096,1024]{1,0:T(8,128)(2,1)} %all-gather.13.cloned.1.call-done), kind=kOutput, calls=%fused_computation.179 | convolution fusion | flops 5771362304 | bytes 16842752 | tf_op jit(solution)/shard_map/sth,hd->std/dot_general | solution.py:14
  699.4 130.8 %all-reduce.5.cloned.1.call-done = (f32[8,16,1024]{2,1,0:T(8,128)}, f32[8,1024,16]{1,2,0:T(8,128)}, f32[8,16,1024]{2,1,0:T(8,128)}, f32[8,4096,16]{1,2,0:T(8,128...) async-done(((f32[8,16,1024]{2,1,0:T(8,128)}, f32[8,1024,16]{1,2,0:T(8,128)}, f32[8,16,1024]{2,1,0:T(8,128)}, f32[8,4096,16]{1,2,0:T(8,128)}, f32[8,16,4096]{2,1,0:T(8,128)}, ...) | async-done | bytes 6291472 | tf_op jit(solution)/shard_map/psum | solution.py:237
  833.7 68.8 %reduce-scatter.5.cloned.1.call-done = f32[1,688,1024]{2,1,0:T(8,128)} async-done(((f32[1,1376,1024]{2,1,0:T(8,128)}), f32[1,688,1024]{2,1,0:T(8,128)}) %reduce-scatter.5.cloned.1.call-update) | async-done | bytes 2818064 | tf_op jit(solution)/shard_map/reduce_scatter | solution.py:228
  910.5 89.8 %all-reduce.7.cloned.1.call-done = (f32[8,3,512,16]{2,3,1,0:T(8,128)}, f32[8,16,512]{2,1,0:T(8,128)}) async-done(((f32[8,3,512,16]{2,3,1,0:T(8,128)}, f32[8,16,512]{2,1,0:T(8,128)}), (f32[8,3,512,16]{2,3,1,0:T(8,128)}, f32[8,16,512]{2,1,0:T(8,128)})) %all-reduce.7.cloned.1.call-update) | async-done | bytes 1048592 | tf_op jit(solution)/shard_map/psum | solution.py:236
  (246 shorter events, 112.5 us)
Async XLA Ops:
  7.2 55.3 %copy-start = (bf16[1024,3,512]{2,0,1:T(8,128)(2,1)S(1)}, bf16[1024,3,512]{2,0,1:T(8,128)(2,1)}, u32[]{:S(2)}) copy-start(bf16[1024,3,512]{2,0,1:T(8,128)(2,1)} %param.28) | copy-start | bytes 9437188
  7.2 50.6 %all-gather.7.cloned.1.call-start = ((), (), s32[]{:S(2)}) async-start(), calls=%async_computation.2 | async-start | bytes 4227072 | tf_op jit(solution)/shard_map/all_gather | solution.py:126
  13.7 155.3 %all-gather.11.cloned.1.call-start = ((), (), s32[]{:S(2)}) async-start(), calls=%async_computation.5 | async-start | bytes 1572864 | tf_op jit(solution)/shard_map/all_gather | solution.py:163
  14.5 178.8 %all-gather.15.cloned.1.call-start = ((), (), s32[]{:S(2)}) async-start(), calls=%async_computation.7 | async-start | bytes 1572864 | tf_op jit(solution)/shard_map/all_gather | solution.py:164
  15.2 193.8 %all-gather.13.cloned.1.call-start = ((), (), s32[]{:S(2)}) async-start(), calls=%async_computation.6 | async-start | bytes 12582912 | tf_op jit(solution)/shard_map/all_gather | solution.py:162
  15.8 265.4 %reduce-scatter.3.cloned.1.call-start = ((), (), s32[]{:S(2)}) async-start(), calls=%async_computation.3 | async-start | bytes 8454144 | tf_op jit(solution)/shard_map/reduce_scatter | solution.py:157
  17.6 139.8 %copy-start.19 = (bf16[1,1024,16]{2,1,0:T(8,128)(2,1)}, bf16[1,1024,16]{2,1,0:T(8,128)(2,1)S(1)}, u32[]{:S(2)}) copy-start(bf16[1,1024,16]{2,1,0:T(8,128)(2,1)S(1)} %copy.76) | copy-start | bytes 98308
  18.8 133.5 %copy-start.52 = (bf16[1,16,512]{2,0,1:T(2,128)(2,1)}, bf16[1,16,512]{2,0,1:T(2,128)(2,1)S(1)}, u32[]{:S(2)}) copy-start(bf16[1,16,512]{2,0,1:T(2,128)(2,1)S(1)} %fusion.79) | copy-start | bytes 49156
  20.0 40.4 %copy-start.37 = (bf16[1,16,1024]{2,0,1:T(2,128)(2,1)}, bf16[1,16,1024]{2,0,1:T(2,128)(2,1)S(1)}, u32[]{:S(2)}) copy-start(bf16[1,16,1024]{2,0,1:T(2,128)(2,1)S(1)} %fusion.77) | copy-start | bytes 98308
  104.1 23.7 %copy-start.34 = (f32[8,1376]{1,0:T(8,128)}, f32[8,1376]{1,0:T(8,128)S(1)}, u32[]{:S(2)}) copy-start(f32[8,1376]{1,0:T(8,128)S(1)} %get-tuple-element.62) | copy-start | bytes 132100
  127.8 24.5 %copy-start.47 = (f32[8,1376]{1,0:T(8,128)}, f32[8,1376]{1,0:T(8,128)S(1)}, u32[]{:S(2)}) copy-start(f32[8,1376]{1,0:T(8,128)S(1)} %fusion.1) | copy-start | bytes 132100
  162.6 224.1 %all-gather.9.cloned.1.call-start = ((), (), s32[]{:S(2)}) async-start(), calls=%async_computation.4 | async-start | bytes 12582912 | tf_op jit(solution)/shard_map/all_gather | solution.py:161
  163.2 331.8 %all-gather.17.cloned.1.call-start = ((), (), s32[]{:S(2)}) async-start(), calls=%async_computation.8 | async-start | bytes 4227072 | tf_op jit(solution)/shard_map/all_gather | solution.py:190
  164.0 16.0 %copy-start.26 = (bf16[1,1024,16]{2,1,0:T(8,128)(2,1)}, bf16[1,1024,16]{2,1,0:T(8,128)(2,1)S(1)}, u32[]{:S(2)}) copy-start(bf16[1,1024,16]{2,1,0:T(8,128)(2,1)S(1)} %copy.84) | copy-start | bytes 98308
  164.6 287.2 %copy-start.58 = (f32[688]{0:T(1024)}, f32[688]{0:T(1024)S(1)}, u32[]{:S(2)}) copy-start(f32[688]{0:T(1024)S(1)} %fusion.85) | copy-start | bytes 8260
  197.3 83.9 %copy-start.71 = (f32[1024]{0:T(1024)S(1)}, f32[1024]{0:T(1024)}, u32[]{:S(2)}) copy-start(f32[1024]{0:T(1024)} %param.26) | copy-start | bytes 12292
  386.7 8.8 copy-start.54
  426.6 23.8 %copy-start.45 = (f32[688,16]{0,1:T(8,128)}, f32[688,16]{0,1:T(8,128)S(1)}, u32[]{:S(2)}) copy-start(f32[688,16]{0,1:T(8,128)S(1)} %fusion.82) | copy-start | bytes 132100
  439.0 8.6 copy-start.70
  453.6 376.6 %all-reduce.5.cloned.1.call-start = ((), (), s32[]{:S(2)}) async-start(), calls=%async_computation.10 | async-start | bytes 12582912 | tf_op jit(solution)/shard_map/psum | solution.py:237
  463.5 31.6 %copy-start.20 = (bf16[1,1024,16]{2,1,0:T(8,128)(2,1)S(1)}, bf16[1,1024,16]{2,1,0:T(8,128)(2,1)}, u32[]{:S(2)}) copy-start(bf16[1,1024,16]{2,1,0:T(8,128)(2,1)} %copy-done.19) | copy-start | bytes 98308
  671.0 231.5 %reduce-scatter.5.cloned.1.call-start = ((), (), s32[]{:S(2)}) async-start(), calls=%async_computation.9 | async-start | bytes 8454144 | tf_op jit(solution)/shard_map/reduce_scatter | solution.py:228
  682.4 317.9 %all-reduce.7.cloned.1.call-start = ((), (), s32[]{:S(2)}) async-start(), calls=%async_computation.11 | async-start | bytes 2097152 | tf_op jit(solution)/shard_map/psum | solution.py:236
  682.5 10.8 %copy-start.3 = (f32[1,688,1024]{2,1,0:T(8,128)S(1)}, f32[1,688,1024]{2,1,0:T(8,128)}, u32[]{:S(2)}) copy-start(f32[1,688,1024]{2,1,0:T(8,128)} %copy-done.1) | copy-start | bytes 8454148
  682.5 10.8 %copy-start.27 = (bf16[1,1024,16]{2,1,0:T(8,128)(2,1)S(1)}, bf16[1,1024,16]{2,1,0:T(8,128)(2,1)}, u32[]{:S(2)}) copy-start(bf16[1,1024,16]{2,1,0:T(8,128)(2,1)} %copy-done.26) | copy-start | bytes 98308
  682.5 10.8 %copy-start.46 = (f32[688,16]{0,1:T(8,128)S(1)}, f32[688,16]{0,1:T(8,128)}, u32[]{:S(2)}) copy-start(f32[688,16]{0,1:T(8,128)} %copy-done.45) | copy-start | bytes 132100
  682.5 10.8 %copy-start.59 = (f32[688]{0:T(1024)S(1)}, f32[688]{0:T(1024)}, u32[]{:S(2)}) copy-start(f32[688]{0:T(1024)} %copy-done.58) | copy-start | bytes 8260
  682.5 10.8 %copy-start.75 = (f32[1024]{0:T(1024)S(1)}, f32[1024]{0:T(1024)}, u32[]{:S(2)}) copy-start(f32[1024]{0:T(1024)} %param.27) | copy-start | bytes 12292
  699.4 203.2 %copy-start.51 = (f32[688]{0:T(1024)S(1)}, f32[688]{0:T(1024)}, u32[]{:S(2)}) copy-start(f32[688]{0:T(1024)} %copy-done.50) | copy-start | bytes 8260
  699.4 203.2 %copy-start.57 = (f32[1024]{0:T(1024)S(1)}, f32[1024]{0:T(1024)}, u32[]{:S(2)}) copy-start(f32[1024]{0:T(1024)} %param.24) | copy-start | bytes 12292
  832.7 72.9 %copy-start.65 = (f32[688]{0:T(1024)S(1)}, f32[688]{0:T(1024)}, u32[]{:S(2)}) copy-start(f32[688]{0:T(1024)} %copy-done.64) | copy-start | bytes 8260
  832.7 73.0 %copy-start.61 = (f32[688]{0:T(1024)S(1)}, f32[688]{0:T(1024)}, u32[]{:S(2)}) copy-start(f32[688]{0:T(1024)} %copy-done.60) | copy-start | bytes 8260
  (54 other events, 180.5 us)
Sparse Core Ops, SparseCore 0:
  13.8 43.9 all-gather.6
  59.3 21.2 all-gather.10
  82.2 21.2 all-gather.14
  105.0 103.9 all-gather.12
  211.2 69.9 reduce-scatter.2
  282.6 103.9 all-gather.8
  453.8 41.2 all-gather.16
  671.1 159.0 all-reduce.4
  832.5 69.9 reduce-scatter.4
  907.0 93.2 all-reduce.6
where the time goes:
time: 1020 us
  waiting for transfers between devices  528 us (52%)
  matrix products  317 us (31%)
  other arithmetic  99.8 us (10%)
  local copies, waits for them, and re-layouts  53.6 us (5%)
  between operations  16.7 us (2%)
    dot_general x38, matrix products, product(): return jnp.einsum(form, left, right, preferred_element_type=jnp.float32)  295 us
    psum x1, waiting for transfers between devices, body(): lax.psum((stack_slots(grad_qkv_a), stack_slots(grad_out_b), stack_slots(g...  131 us
    all_gather x1, waiting for transfers between devices, body(): lax.all_gather(w_up, 'tensor', axis=1, tiled=True)  99.1 us
    psum x1, waiting for transfers between devices, body(): lax.psum((stack_slots(grad_qkv_b), stack_slots(grad_out_a)), 'dp')  89.8 us
    reduce_scatter x1, waiting for transfers between devices, body(): lax.psum_scatter(grad_one_terms, 'tensor', scatter_dimension=1, tiled=True)  68.8 us
    reduce_scatter x1, waiting for transfers between devices, body(): lax.psum_scatter(attn_terms, 'tensor', scatter_dimension=1, tiled=True)  60.7 us
    convert_element_type x1, other arithmetic, attend_back(): grad_scores = (soft * (grad_soft - jnp.sum(soft * grad_soft, axis=-1, kee...  49 us
    all_gather x1, waiting for transfers between devices, body(): full_one = lax.all_gather(normed_one, 'tensor', axis=1, tiled=True)  35.8 us
  transfers between devices with their start and end apart: 10, of which 8 were waited for; matrix products, arithmetic and copies ran while one was open for 21% of the time, Pallas kernels for 0%

commit v1 on v0

--- a/solution.py
+++ b/solution.py
@@ -235,15 +235,18 @@
     grad_up_a, grad_up_b, grad_down_a, grad_down_b = ffn_grads
     sum_qkv_b, sum_out_a = lax.psum((stack_slots(grad_qkv_b), stack_slots(grad_out_a)), "dp")
     joint_sums = lax.psum(
-        (
-            stack_slots(grad_qkv_a),
-            stack_slots(grad_out_b),
-            stack_slots(grad_up_a),
-            stack_slots(grad_up_b),
-            stack_slots(grad_down_a),
-            stack_slots(grad_down_b),
+        lax.psum(
+            (
+                stack_slots(grad_qkv_a),
+                stack_slots(grad_out_b),
+                stack_slots(grad_up_a),
+                stack_slots(grad_up_b),
+                stack_slots(grad_down_a),
+                stack_slots(grad_down_b),
+            ),
+            "tensor",
         ),
-        ("dp", "tensor"),
+        "dp",
     )
     sum_qkv_a, sum_out_b, sum_up_a, up_b_whole, down_a_whole, sum_down_b = joint_sums
     width_local = w_up.shape[1]

time: 1020 us -> 1090 us (1.069)
  waiting for transfers between devices: 528 us -> 583 us
  matrix products: 317 us -> 332 us
    psum x1, waiting for transfers between devices: 89.8 us -> 138 us  [body(): lax.psum(lax.psum((stack_slots(grad_qkv_a), stack_slots(grad_out_b), stac...]
    psum x1, waiting for transfers between devices: 131 us -> 149 us  [body(): lax.psum((stack_slots(grad_qkv_a), stack_slots(grad_out_b), stack_slots(g...]
    dot_general x38, matrix products: 295 us -> 309 us  [product(): return jnp.einsum(form, left, right, preferred_element_type=jnp.float32)]
    all_gather x1, waiting for transfers between devices: 11.8 us -> 0.8 us  [body(): lax.all_gather(w_down, 'tensor', axis=0, tiled=True)]
  transfers between devices with their start and end apart: 10 -> 10, of which waited for: 8 -> 8; matrix products, arithmetic and copies ran while one was open for 21% -> 20% of each run, Pallas kernels for 0% -> 0%
where the time goes in v1:
time: 1090 us; the launch traced here: 1080 us
  waiting for transfers between devices  583 us (53%)
  matrix products  332 us (30%)
  other arithmetic  99.8 us (9%)
  local copies, waits for them, and re-layouts  50 us (5%)
  between operations  16.6 us (2%)
    dot_general x38, matrix products, product(): return jnp.einsum(form, left, right, preferred_element_type=jnp.float32)  309 us
    psum x1, waiting for transfers between devices, body(): lax.psum((stack_slots(grad_qkv_a), stack_slots(grad_out_b), stack_slots(g...  149 us
    psum x1, waiting for transfers between devices, body(): lax.psum(lax.psum((stack_slots(grad_qkv_a), stack_slots(grad_out_b), stac...  138 us
    all_gather x1, waiting for transfers between devices, body(): lax.all_gather(w_up, 'tensor', axis=1, tiled=True)  99.1 us
    reduce_scatter x1, waiting for transfers between devices, body(): lax.psum_scatter(grad_one_terms, 'tensor', scatter_dimension=1, tiled=True)  68.7 us
    reduce_scatter x1, waiting for transfers between devices, body(): lax.psum_scatter(attn_terms, 'tensor', scatter_dimension=1, tiled=True)  60.7 us
    convert_element_type x1, other arithmetic, attend_back(): grad_scores = (soft * (grad_soft - jnp.sum(soft * grad_soft, axis=-1, kee...  49 us
    all_gather x1, waiting for transfers between devices, body(): full_one = lax.all_gather(normed_one, 'tensor', axis=1, tiled=True)  35.8 us
  transfers between devices with their start and end apart: 10, of which 8 were waited for; matrix products, arithmetic and copies ran while one was open for 20% of the time, Pallas kernels for 0%

profile of v1, /device:TPU:0, one launch (start us, length us, event | category | flops | bytes accessed | tf_op | source)
XLA Modules:
  0.0 1082.3 jit_solution(14175524826322393596)
XLA Ops:
  22.0 35.8 %all-gather.7.cloned.1.call-done = bf16[1,1376,1024]{2,1,0:T(8,128)(2,1)} async-done(((bf16[1,688,1024]{2,1,0:T(8,128)(2,1)}), bf16[1,1376,1024]{2,1,0:T(8,128)(2,1)}) %all-gather.7.cloned.1.call-update) | async-done | bytes 2818064 | tf_op jit(solution)/shard_map/all_gather | solution.py:126
  62.9 5.4 fusion.23
  78.0 25.8 %fusion.116 = (f32[8,1376]{1,0:T(8,128)S(1)}, f32[8,1376,1376]{1,2,0:T(8,128)}) fusion(bf16[1376,8,64]{0,2,1:T(8,128)(2,1)} %bitcast.204, bf16[1376,8,64]{0,2,1:T(8,128)(2,1)} %bitcast.202, pred[1376]{0:T(1024)(128)(4,1)S(1)} %iota_compare_fusion), kind=kOutput, calls=%fused_computation.176 | convolution fusion | flops 1984247040 | bytes 63451488 | tf_op jit(solution)/shard_map/while/body/eval_jaxpr/qhe,khe->hqk/dot_general | solution.py:14
  103.9 23.7 %fusion.1 = f32[8,1376]{1,0:T(8,128)S(1)} fusion(f32[8,1376,1376]{1,2,0:T(8,128)} %get-tuple-element.69, f32[8,1376]{1,0:T(8,128)S(1)} %get-tuple-element.68), kind=kLoop, calls=%fused_computation.7 | loop fusion | flops 30283008 | bytes 60676096 | tf_op jit(solution)/shard_map/while/body/eval_jaxpr/reduce_sum | solution.py:147
  127.6 35.6 %fusion.35 = bf16[8,64,1376]{2,1,0:T(8,128)(2,1)} fusion(bf16[1376,8,64]{0,2,1:T(8,128)(2,1)} %bitcast.214, f32[8,1376,1376]{1,2,0:T(8,128)} %get-tuple-element.69, f32[8,1376]{1,0:T(8,128)S(1)} %fusion.1, f32[8,1376]{1,0:T(8,128)S(1)} %get-tuple-element.68), kind=kOutput, calls=%fused_computation.61 | convolution fusion | flops 1984962560 | bytes 63494144 | tf_op jit(solution)/shard_map/while/body/eval_jaxpr/hqk,khe->qhe/dot_general | solution.py:14
  164.9 3.4 fusion.117
  168.3 5.2 add_bitcast_fusion
  179.9 11.0 %fusion.67 = bf16[1,4096,16]{0,1,2:T(8,128)(2,1)} fusion(bf16[8,4096,16]{1,2,0:T(8,128)(2,1)} %all-gather.11.cloned.1.call-done, s32[]{:T(128)} %bitcast.198), kind=kOutput, calls=%fused_computation.100 | convolution fusion | flops 1048584 | bytes 1179652 | tf_op jit(solution)/shard_map/sn,n...->s.../dot_general | solution.py:14
  190.9 13.3 %copy.80 = bf16[1,4096,16]{1,2,0:T(8,128)(2,1)S(1)} copy(bf16[1,4096,16]{0,1,2:T(8,128)(2,1)} %fusion.67) | data formatting | bytes 262144 | tf_op jit(solution)/shard_map/sn,n...->s.../dot_general | solution.py:14
  209.0 11.4 %fusion.108 = f32[688,4096]{1,0:T(8,128)} fusion(bf16[4096,1024]{1,0:T(8,128)(2,1)} %all-gather.13.cloned.1.call-done, bf16[1,688,1024]{2,1,0:T(8,128)(2,1)} %param.21, f32[1024]{0:T(1024)S(1)} %copy-done.71, f32[688]{0:T(1024)S(1)} %fusion.85), kind=kOutput, calls=%fused_computation.169 | convolution fusion | flops 5774180352 | bytes 21076672 | tf_op jit(solution)/shard_map/std,hd->sth/dot_general | solution.py:14
  220.4 60.7 %reduce-scatter.3.cloned.1.call-done = f32[1,688,1024]{2,1,0:T(8,128)} async-done(((f32[1,1376,1024]{2,1,0:T(8,128)}), f32[1,688,1024]{2,1,0:T(8,128)}) %reduce-scatter.3.cloned.1.call-update) | async-done | bytes 2818064 | tf_op jit(solution)/shard_map/reduce_scatter | solution.py:157
  287.5 99.1 %all-gather.9.cloned.1.call-done = bf16[1024,4096]{1,0:T(8,128)(2,1)} async-done(((bf16[1024,2048]{1,0:T(8,128)(2,1)}), bf16[1024,4096]{1,0:T(8,128)(2,1)}) %all-gather.9.cloned.1.call-update) | async-done | bytes 8388624 | tf_op jit(solution)/shard_map/all_gather | solution.py:161
  386.7 8.8 fusion.118
  395.5 28.7 %fusion.9 = (bf16[688,4096]{1,0:T(8,128)(2,1)S(1)}, f32[688,4096]{1,0:T(8,128)}) fusion(f32[688,4096]{1,0:T(8,128)S(1)} %fusion.118, bf16[688,16]{0,1:T(8,128)(2,1)S(1)} %copy-done.51, bf16[1,4096,16]{1,2,0:T(8,128)(2,1)S(1)} %copy.80), kind=kOutput, calls=%fused_computation.16 | convolution fusion | flops 276168704 | bytes 28333568 | tf_op jit(solution)/shard_map/str,shr->sth/dot_general | solution.py:14
  426.5 10.0 fusion.15
  438.9 8.6 fusion.120
  456.4 3.5 fusion.123
  459.9 4.1 fusion.124
  467.1 28.4 %all-gather.17.cloned.1.call-done = bf16[1,1376,1024]{2,1,0:T(8,128)(2,1)} async-done(((bf16[1,688,1024]{2,1,0:T(8,128)(2,1)}), bf16[1,1376,1024]{2,1,0:T(8,128)(2,1)}) %all-gather.17.cloned.1.call-update) | async-done | bytes 2818064 | tf_op jit(solution)/shard_map/all_gather | solution.py:190
  505.5 23.2 %fusion.29 = bf16[8,64,1376]{2,1,0:T(8,128)(2,1)} fusion(bf16[1376,8,64]{0,2,1:T(8,128)(2,1)} %bitcast.206, f32[8,1376,1376]{1,2,0:T(8,128)} %get-tuple-element.69, f32[8,1376]{1,0:T(8,128)S(1)} %copy-done.14), kind=kOutput, calls=%fused_computation.57 | convolution fusion | flops 1969815552 | bytes 63450112 | tf_op jit(solution)/shard_map/while/body/eval_jaxpr/hqk,qhe->khe/dot_general | solution.py:14
  528.7 43.6 %multiply_reduce_fusion = (f32[8,1376]{1,0:T(8,128)S(1)}, f32[8,1376,1376]{1,2,0:T(8,128)}) fusion(f32[8,1376,1376]{1,2,0:T(8,128)} %get-tuple-element.69, f32[8,1376]{1,0:T(8,128)S(1)} %copy-done.14, bf16[1376,8,64]{0,2,1:T(8,128)(2,1)} %bitcast.207, bf16[1376,8,64]{0,2,1:T(8,128)(2,1)} %bitcast.215), kind=kOutput, calls=%fused_computation.3 | convolution fusion | flops 1984247040 | bytes 124082176 | tf_op jit(solution)/shard_map/while/body/eval_jaxpr/qhe,khe->hqk/dot_general | solution.py:14
  572.2 49.0 %multiply_convert_fusion = bf16[8,1376,1376]{1,2,0:T(8,128)(2,1)} fusion(f32[8,1376,1376]{1,2,0:T(8,128)} %get-tuple-element.75, f32[8,1376,1376]{1,2,0:T(8,128)} %get-tuple-element.69, f32[8,1376]{1,0:T(8,128)S(1)} %get-tuple-element.74, f32[8,1376]{1,0:T(8,128)S(1)} %copy-done.14), kind=kLoop, calls=%fused_computation.2 | loop fusion | flops 60588032 | bytes 151558144 | tf_op jit(solution)/shard_map/while/body/eval_jaxpr/convert_element_type | solution.py:212
  621.2 16.6 %fusion.34 = bf16[8,64,1376]{2,1,0:T(8,128)(2,1)} fusion(bf16[1376,8,64]{0,2,1:T(8,128)(2,1)} %bitcast.205, bf16[8,1376,1376]{1,2,0:T(8,128)(2,1)} %multiply_convert_fusion), kind=kOutput, calls=%fused_computation.60 | convolution fusion | flops 1940226048 | bytes 33112064 | tf_op jit(solution)/shard_map/while/body/eval_jaxpr/hqk,qhe->khe/dot_general | solution.py:14
  637.8 16.5 %fusion.33 = bf16[8,64,1376]{2,1,0:T(8,128)(2,1)} fusion(bf16[1376,8,64]{0,2,1:T(8,128)(2,1)} %bitcast.203, bf16[8,1376,1376]{1,2,0:T(8,128)(2,1)} %multiply_convert_fusion), kind=kOutput, calls=%fused_computation.59 | convolution fusion | flops 1940226048 | bytes 33112064 | tf_op jit(solution)/shard_map/while/body/eval_jaxpr/hqk,khe->qhe/dot_general | solution.py:14
  662.0 3.1 fusion.40
  677.6 148.9 %all-reduce.7.cloned.1.call-done = (f32[8,16,1024]{2,1,0:T(8,128)}, f32[8,1024,16]{1,2,0:T(8,128)}, f32[8,16,1024]{2,1,0:T(8,128)}, f32[8,4096,16]{1,2,0:T(8,128...) async-done(((f32[8,16,1024]{2,1,0:T(8,128)}, f32[8,1024,16]{1,2,0:T(8,128)}, f32[8,16,1024]{2,1,0:T(8,128)}, f32[8,4096,16]{1,2,0:T(8,128)}, f32[8,16,4096]{2,1,0:T(8,128)}, ...) | async-done | bytes 6291472 | tf_op jit(solution)/shard_map/psum | solution.py:238
  826.7 6.6 fusion.111
  833.2 5.0 fusion.24
  838.3 10.4 fusion.119
  851.7 138.4 %all-reduce.5.cloned.1.call-done = (f32[8,16,1024]{2,1,0:T(8,128)}, f32[8,3,512,16]{2,3,1,0:T(8,128)}, f32[8,16,512]{2,1,0:T(8,128)}, f32[8,1024,16]{1,2,0:T(8,1...) async-done(((f32[8,16,1024]{2,1,0:T(8,128)}, f32[8,3,512,16]{2,3,1,0:T(8,128)}, ...) | async-done | bytes 7340048 | tf_op jit(solution)/shard_map/psum | solution.py:237
  993.6 68.7 %reduce-scatter.5.cloned.1.call-done = f32[1,688,1024]{2,1,0:T(8,128)} async-done(((f32[1,1376,1024]{2,1,0:T(8,128)}), f32[1,688,1024]{2,1,0:T(8,128)}) %reduce-scatter.5.cloned.1.call-update) | async-done | bytes 2818064 | tf_op jit(solution)/shard_map/reduce_scatter | solution.py:228
  1062.3 3.0 fusion.39
  (242 shorter events, 110.4 us)
Async XLA Ops:
  7.2 55.2 %copy-start = (bf16[1024,3,512]{2,0,1:T(8,128)(2,1)S(1)}, bf16[1024,3,512]{2,0,1:T(8,128)(2,1)}, u32[]{:S(2)}) copy-start(bf16[1024,3,512]{2,0,1:T(8,128)(2,1)} %param.28) | copy-start | bytes 9437188
  7.2 50.6 %all-gather.7.cloned.1.call-start = ((), (), s32[]{:S(2)}) async-start(), calls=%async_computation.2 | async-start | bytes 4227072 | tf_op jit(solution)/shard_map/all_gather | solution.py:126
  13.7 166.2 %all-gather.11.cloned.1.call-start = ((), (), s32[]{:S(2)}) async-start(), calls=%async_computation.5 | async-start | bytes 1572864 | tf_op jit(solution)/shard_map/all_gather | solution.py:163
  14.5 189.8 %all-gather.15.cloned.1.call-start = ((), (), s32[]{:S(2)}) async-start(), calls=%async_computation.7 | async-start | bytes 1572864 | tf_op jit(solution)/shard_map/all_gather | solution.py:164
  15.2 193.8 %all-gather.13.cloned.1.call-start = ((), (), s32[]{:S(2)}) async-start(), calls=%async_computation.6 | async-start | bytes 12582912 | tf_op jit(solution)/shard_map/all_gather | solution.py:162
  15.8 265.4 %reduce-scatter.3.cloned.1.call-start = ((), (), s32[]{:S(2)}) async-start(), calls=%async_computation.3 | async-start | bytes 8454144 | tf_op jit(solution)/shard_map/reduce_scatter | solution.py:157
  17.6 150.7 %copy-start.18 = (bf16[1,1024,16]{2,1,0:T(8,128)(2,1)}, bf16[1,1024,16]{2,1,0:T(8,128)(2,1)S(1)}, u32[]{:S(2)}) copy-start(bf16[1,1024,16]{2,1,0:T(8,128)(2,1)S(1)} %copy.76) | copy-start | bytes 98308
  18.8 144.4 %copy-start.49 = (bf16[1,16,512]{2,0,1:T(2,128)(2,1)}, bf16[1,16,512]{2,0,1:T(2,128)(2,1)S(1)}, u32[]{:S(2)}) copy-start(bf16[1,16,512]{2,0,1:T(2,128)(2,1)S(1)} %fusion.79) | copy-start | bytes 49156
  20.0 40.4 %copy-start.33 = (bf16[1,16,1024]{2,0,1:T(2,128)(2,1)}, bf16[1,16,1024]{2,0,1:T(2,128)(2,1)S(1)}, u32[]{:S(2)}) copy-start(bf16[1,16,1024]{2,0,1:T(2,128)(2,1)S(1)} %fusion.77) | copy-start | bytes 98308
  103.9 23.7 %copy-start.32 = (f32[8,1376]{1,0:T(8,128)}, f32[8,1376]{1,0:T(8,128)S(1)}, u32[]{:S(2)}) copy-start(f32[8,1376]{1,0:T(8,128)S(1)} %get-tuple-element.68) | copy-start | bytes 132100
  127.6 35.6 %copy-start.44 = (f32[8,1376]{1,0:T(8,128)}, f32[8,1376]{1,0:T(8,128)S(1)}, u32[]{:S(2)}) copy-start(f32[8,1376]{1,0:T(8,128)S(1)} %fusion.1) | copy-start | bytes 132100
  173.5 213.2 %all-gather.9.cloned.1.call-start = ((), (), s32[]{:S(2)}) async-start(), calls=%async_computation.4 | async-start | bytes 12582912 | tf_op jit(solution)/shard_map/all_gather | solution.py:161
  174.1 321.5 %all-gather.17.cloned.1.call-start = ((), (), s32[]{:S(2)}) async-start(), calls=%async_computation.8 | async-start | bytes 4227072 | tf_op jit(solution)/shard_map/all_gather | solution.py:190
  174.9 16.1 %copy-start.22 = (bf16[1,1024,16]{2,1,0:T(8,128)(2,1)}, bf16[1,1024,16]{2,1,0:T(8,128)(2,1)S(1)}, u32[]{:S(2)}) copy-start(bf16[1,1024,16]{2,1,0:T(8,128)(2,1)S(1)} %copy.84) | copy-start | bytes 98308
  175.5 276.9 %copy-start.55 = (f32[688]{0:T(1024)}, f32[688]{0:T(1024)S(1)}, u32[]{:S(2)}) copy-start(f32[688]{0:T(1024)S(1)} %fusion.85) | copy-start | bytes 8260
  208.2 72.9 %copy-start.69 = (f32[1024]{0:T(1024)S(1)}, f32[1024]{0:T(1024)}, u32[]{:S(2)}) copy-start(f32[1024]{0:T(1024)} %param.26) | copy-start | bytes 12292
  386.7 8.8 copy-start.51
  426.5 23.9 %copy-start.42 = (f32[688,16]{0,1:T(8,128)}, f32[688,16]{0,1:T(8,128)S(1)}, u32[]{:S(2)}) copy-start(f32[688,16]{0,1:T(8,128)S(1)} %fusion.82) | copy-start | bytes 132100
  438.9 8.6 copy-start.68
  454.1 372.4 %all-reduce.7.cloned.1.call-start = ((), (), s32[]{:S(2)}) async-start(), calls=%async_computation.11 | async-start | bytes 12582912 | tf_op jit(solution)/shard_map/psum | solution.py:238
  464.0 31.6 %copy-start.19 = (bf16[1,1024,16]{2,1,0:T(8,128)(2,1)S(1)}, bf16[1,1024,16]{2,1,0:T(8,128)(2,1)}, u32[]{:S(2)}) copy-start(bf16[1,1024,16]{2,1,0:T(8,128)(2,1)} %copy-done.18) | copy-start | bytes 98308
  671.3 318.7 %all-reduce.5.cloned.1.call-start = ((), (), s32[]{:S(2)}) async-start(), calls=%async_computation.10 | async-start | bytes 14680064 | tf_op jit(solution)/shard_map/psum | solution.py:237
  826.6 235.7 %reduce-scatter.5.cloned.1.call-start = ((), (), s32[]{:S(2)}) async-start(), calls=%async_computation.9 | async-start | bytes 8454144 | tf_op jit(solution)/shard_map/reduce_scatter | solution.py:228
  838.2 10.5 copy-start.3
  838.3 10.5 copy-start.23
  838.3 10.5 copy-start.43
  838.3 10.5 copy-start.56
  838.3 10.5 copy-start.73
  851.7 210.6 %copy-start.48 = (f32[688]{0:T(1024)S(1)}, f32[688]{0:T(1024)}, u32[]{:S(2)}) copy-start(f32[688]{0:T(1024)} %copy-done.47) | copy-start | bytes 8260
  990.1 72.2 %copy-start.54 = (f32[1024]{0:T(1024)S(1)}, f32[1024]{0:T(1024)}, u32[]{:S(2)}) copy-start(f32[1024]{0:T(1024)} %param.24) | copy-start | bytes 12292
  992.5 72.8 %copy-start.63 = (f32[688]{0:T(1024)S(1)}, f32[688]{0:T(1024)}, u32[]{:S(2)}) copy-start(f32[688]{0:T(1024)} %copy-done.62) | copy-start | bytes 8260
  992.5 72.8 %copy-start.58 = (f32[688]{0:T(1024)S(1)}, f32[688]{0:T(1024)}, u32[]{:S(2)}) copy-start(f32[688]{0:T(1024)} %copy-done.57) | copy-start | bytes 8260
  (52 other events, 162.7 us)
Sparse Core Ops, SparseCore 0:
  13.8 43.9 all-gather.6
  59.3 21.2 all-gather.10
  82.2 21.2 all-gather.14
  105.0 103.9 all-gather.12
  211.2 69.9 reduce-scatter.2
  282.6 103.9 all-gather.8
  454.3 41.2 all-gather.16
  671.5 155.0 all-reduce.6
  832.5 157.5 all-reduce.4
  992.3 69.9 reduce-scatter.4
